TPU v7x, 32 devices: a whole 2x2x4 slice. The times are simulated.
32 devices in a mesh: space: 8 (over z, x), mem: 4 (over y, core).
Axes of the slice: x: 2, y: 2, z: 4, core: 2. Of those that a mesh axis runs over, the one named last changes fastest.
Arguments:
- ensemble_state: bfloat16 [256, 512, 256], P('mem', 'space'), may hold values from -6 to 6
- obs_ens: bfloat16 [256, 512, 128], P('mem', 'space'), may hold values from -6 to 6
- innovation: float32 [512, 128], P('space'), may hold values from -6 to 6
- obs_prec: float32 [512, 128], P('space'), may hold values from 0.25 to 2
- block_list: int32 [512, 8], P('space'), may hold values from 0 to 511, as said below
- block_count: int32 [512], P('space'), may hold values from 1 to 8
- loc_weight: float32 [512, 8], P('space'), may hold values from 0.1 to 1
- prior_weight: float32 [512, 256], P('space'), may hold values from 0.1 to 10, as said below
Outputs:
- analysis: bfloat16 [256, 512, 256], P('mem', 'space')
Inputs may be any that keep to these rules, and one draw needn't show every extreme that they name: `block_list`: among the 128 entries of the regions r with the same r // 16, at most 24 name blocks b with the same b // 64, and exactly 24 do for one such value. `prior_weight`: Positive.
All inputs are finite; a program needn't handle non-finite values.
Results may differ from a plain program's by a relative error of at most 0.012.
Values may be sent and summed in bfloat16 or wider, within the bound.
No kernel may reach another device: no remote copies, remote signals or barrier semaphores. Data moves between devices by JAX's collectives and lax.ppermute only.
A program may use at most 128 MiB of HBM per device.

v0:
```python
import functools

import jax
import jax.numpy as jnp
from jax import lax
from jax.experimental import pallas as pl
from jax.experimental.pallas import tpu as pltpu
from jax.sharding import PartitionSpec as P

INFLATION = 1.1
PANEL = 32
GROUP = 4
LANES = 128
CHUNKS = (2, 2)
SPLIT = 2
F32 = jnp.float32
BF16 = jnp.bfloat16
NT = (((1,), (1,)), ((), ()))


def split3(value):
    high = value.astype(BF16)
    rest = value - high.astype(F32)
    mid = rest.astype(BF16)
    low = (rest - mid.astype(F32)).astype(BF16)
    return high, mid, low


def weights_kernel(ids_ref, local_ref, *rest):
    part_refs, (out_ref, rows_ref) = rest[:-2], rest[-2:]
    width = out_ref.shape[1] // 2
    size = part_refs[0].shape[0]
    for index, part_ref in enumerate(part_refs):
        rows_ref[index * size : (index + 1) * size] = part_ref[...]

    @pl.loop(0, out_ref.shape[0] // 8, unroll=4)
    def _(group):
        prec, innov = [], []
        for inside in range(8):
            entry = group * 8 + inside
            row = rows_ref[pl.ds(ids_ref[entry], 1), :]
            prec.append(local_ref[entry] * row[:, :width])
            innov.append(row[:, width:])
        scale = jnp.sqrt(jnp.concatenate(prec, axis=0))
        first = pl.multiple_of(group * 8, 8)
        out_ref[pl.ds(first, 8), :width] = scale
        out_ref[pl.ds(first, 8), width:] = scale * jnp.concatenate(innov, axis=0)


def weights(ids, local, parts):
    smem = pl.BlockSpec(memory_space=pltpu.SMEM)
    vmem = pl.BlockSpec(memory_space=pltpu.VMEM)
    size, length = parts[0].shape
    return pl.pallas_call(
        weights_kernel,
        out_shape=jax.ShapeDtypeStruct((ids.shape[0], length), F32),
        in_specs=[smem, smem] + [vmem] * len(parts),
        out_specs=vmem,
        scratch_shapes=[pltpu.VMEM((len(parts) * size, length), F32)],
    )(ids, local, *parts)


def pick_kernel(layout, group_size, first_region, regions, ids_ref, scale_ref, *rest):
    shard_refs, (out_ref, table_ref) = rest[:-2], rest[-2:]
    width = table_ref.shape[2]
    slots = out_ref.shape[1] // regions
    for shard_ref, (start, size) in zip(shard_refs, layout):
        table_ref[start : start + size] = shard_ref[...]

    for member in range(out_ref.shape[0]):

        @pl.loop(0, regions)
        def _(region):
            first = (member * group_size + first_region + region) * slots
            first = pl.multiple_of(first, slots)
            scales = scale_ref[pl.ds(first, slots), :width]
            for slot in range(slots):
                values = table_ref[ids_ref[first + slot]].astype(F32)
                out_ref[member, region * slots + slot] = (
                    values * scales[slot : slot + 1]
                ).astype(BF16)


def pick(ids, scales, shards, mem_count, group_size, first_region, regions):
    slots = ids.shape[0] // (mem_count * group_size)
    layout = []
    total = 0
    for shard in shards:
        layout.append((total, shard.shape[0]))
        total += shard.shape[0]
    row, dtype = shards[0].shape[1:], shards[0].dtype
    entries = regions * slots
    size = row[0] * row[1]
    return pl.pallas_call(
        functools.partial(pick_kernel, layout, group_size, first_region, regions),
        out_shape=jax.ShapeDtypeStruct((mem_count, entries) + row, dtype),
        in_specs=[
            pl.BlockSpec(memory_space=pltpu.SMEM),
        ]
        + [pl.BlockSpec(memory_space=pltpu.VMEM)] * (1 + len(shards)),
        out_specs=pl.BlockSpec(memory_space=pltpu.VMEM),
        scratch_shapes=[pltpu.VMEM((total,) + row, dtype)],
        cost_estimate=pl.CostEstimate(
            flops=mem_count * entries * size,
            bytes_accessed=4 * (mem_count * entries + total) * size,
            transcendentals=0,
        ),
        compiler_params=pltpu.CompilerParams(vmem_limit_bytes=24 << 20),
    )(ids, scales, *shards)


def grid_cycle(outer, inner):
    cells = []
    for row in range(outer):
        columns = range(1, inner) if row % 2 == 0 else range(inner - 1, 0, -1)
        cells += [row * inner + column for column in columns]
    return cells + [row * inner for row in range(outer - 1, -1, -1)]


def row_stack(rows, count):
    length = rows[0].shape[1]
    which = lax.broadcasted_iota(jnp.int32, (count, length), 0)
    stack = jnp.zeros((count, length), F32)
    for index, row in enumerate(rows):
        stack = jnp.where(which == index, row.astype(F32), stack)
    return stack.astype(BF16)


def region_setup(
    region, first, prior_ref, column_ref, weight_ref, states_ref, obs_refs, scaled_ref,
    work_ref, mean_ref,
):
    members = prior_ref.shape[1]
    sources, members_dev = states_ref.shape[0], states_ref.shape[2]
    points = states_ref.shape[3]
    slots = obs_refs[0].shape[1] // prior_ref.shape[0]
    width = obs_refs[0].shape[3]
    for slot in range(slots):
        for source in range(sources):
            start = source * members_dev
            for obs_ref in obs_refs:
                stop = start + obs_ref.shape[2]
                scaled_ref[start:stop, slot * width : (slot + 1) * width] = (
                    obs_ref[source, region * slots + slot]
                )
                start = stop
    scaled = scaled_ref[...]
    gram = lax.dot_general(scaled, scaled, NT, preferred_element_type=F32)
    prior_row = prior_ref[pl.ds(region, 1), :]
    whole = 1.0 / jnp.sum(prior_row, axis=1, keepdims=True)
    share_row = prior_row * whole
    share_col = column_ref[region] * whole
    root_row = jnp.sqrt(members * share_row)
    root_col = jnp.sqrt(members * share_col)
    average = jnp.sum(
        jnp.dot(
            row_stack(split3(share_row), 16), scaled, preferred_element_type=F32
        ),
        axis=0, keepdims=True,
    )
    own = weight_ref[pl.ds(pl.multiple_of(first + region * slots, slots), slots), width:]
    innov = jnp.concatenate([own[slot : slot + 1] for slot in range(slots)], axis=1)
    sums = lax.dot_general(
        scaled, row_stack(split3(innov) + split3(average), 16), NT,
        preferred_element_type=F32,
    )
    kind = lax.broadcasted_iota(jnp.int32, (16, 2 * LANES), 0) // 3
    side = lax.broadcasted_iota(jnp.int32, (16, 2 * LANES), 1) // LANES
    spread = jnp.where(kind == side, 1.0, 0.0).astype(BF16)
    sums = sum(
        jnp.dot(part, spread, preferred_element_type=F32) for part in split3(sums)
    )
    projection, left_col = sums[:, :LANES], sums[:, LANES:]
    total = jnp.sum(share_col * left_col, axis=0, keepdims=True)
    left_col = left_col - total
    vector = root_col * (
        projection - jnp.sum(share_col * projection, axis=0, keepdims=True)
    )
    work_ref[region, :, members + points :] = vector
    for start in range(0, members, LANES):
        tile = slice(start, start + LANES)
        part = gram[:, tile]
        left_row = jnp.sum(share_col * part, axis=0, keepdims=True)
        system = root_col * ((part - left_row) - left_col) * root_row[:, tile]
        on_diag = lax.broadcasted_iota(jnp.int32, (members, LANES), 0) == (
            lax.broadcasted_iota(jnp.int32, (members, LANES), 1) + start
        )
        work_ref[region, :, tile] = system + jnp.where(
            on_diag, (members - 1) / INFLATION, 0.0
        )
    for start in range(0, points, LANES):
        states = jnp.concatenate(
            [
                states_ref[source, region, :, start : start + LANES].astype(F32)
                for source in range(sources)
            ],
            axis=0,
        )
        mean = jnp.sum(share_col * states, axis=0, keepdims=True)
        mean_ref[region, :, start : start + LANES] = jnp.broadcast_to(mean, (8, LANES))
        work_ref[region, :, members + start : members + start + LANES] = root_col * (
            states - mean
        )


def reciprocal(value):
    guess = pl.reciprocal(value, approx=True)
    guess = guess * (2.0 - value * guess)
    return guess * (2.0 - value * guess)


def factor_diagonals(panel, chosen, work_ref):
    per_pack = LANES // PANEL
    start = panel * PANEL
    base, offset = start // LANES * LANES, start % LANES
    lane = lax.broadcasted_iota(jnp.int32, (8, LANES), 1)
    sub = lax.broadcasted_iota(jnp.int32, (8, LANES), 0)
    owner, column = lane // PANEL, lane % PANEL
    tiles = PANEL // 8
    packs = len(chosen)
    blocks = []
    for pack in chosen:
        pieces = []
        for tile in range(tiles):
            merged = None
            for place in range(per_pack):
                region = pack * per_pack + place
                raw = work_ref[
                    region, start + 8 * tile : start + 8 * tile + 8, base : base + LANES
                ]
                shift = (place * PANEL - offset) % LANES
                if shift:
                    raw = pltpu.roll(raw, shift, axis=1)
                merged = raw if merged is None else jnp.where(owner == place, raw, merged)
            pieces.append(merged)
        blocks.append(pieces)
    pivots = [[jnp.ones((8, LANES), F32) for _ in range(tiles)] for _ in range(packs)]
    for first in range(0, PANEL, GROUP):
        home = first // 8
        columns = [
            [
                {
                    tile: jnp.take_along_axis(
                        blocks[pack][tile], owner * PANEL + first + step,
                        axis=1, mode="promise_in_bounds",
                    )
                    for tile in range(home, tiles)
                }
                for step in range(GROUP)
            ]
            for pack in range(packs)
        ]
        second = {}
        for step in range(GROUP):
            inside = first % 8 + step
            at_step = column == first + step
            below = sub > inside
            for pack in range(packs):
                pieces = blocks[pack]
                if step % 2 == 0:
                    pivot = columns[pack][step][home][inside : inside + 1, :]
                    cross = columns[pack][step + 1][home][inside : inside + 1, :]
                    other = columns[pack][step + 1][home][inside + 1 : inside + 2, :]
                    product = pivot * other - cross * cross
                    inverse = reciprocal(pivot)
                    second[pack] = product * inverse, pivot * reciprocal(product)
                else:
                    pivot, inverse = second[pack]
                row = jnp.where(at_step[:1], 1.0, pieces[home][inside : inside + 1, :])
                pivots[pack][home] = jnp.where(sub == inside, pivot, pivots[pack][home])
                later = {
                    other: columns[pack][other][home][inside : inside + 1, :]
                    for other in range(step + 1, GROUP)
                }
                for tile in range(home, tiles):
                    ratio = columns[pack][step][tile] * inverse
                    cleared = at_step
                    if tile == home:
                        ratio = jnp.where(below, ratio, 0.0)
                        cleared = at_step & below
                    for other in later:
                        columns[pack][other][tile] = (
                            columns[pack][other][tile] - ratio * later[other]
                        )
                    pieces[tile] = jnp.where(cleared, 0.0, pieces[tile]) - ratio * row
    results = []
    for pack in range(packs):
        rows = []
        for tile in range(tiles):
            index = sub + 8 * tile
            lower = jnp.where(
                column < index, blocks[pack][tile], jnp.where(column == index, 1.0, 0.0)
            )
            rows.append(lower * lax.rsqrt(pivots[pack][tile]))
        results.append(jnp.concatenate(rows, axis=0))
    return results


def six_products(left, right, axis):
    high, mid, low = left
    left = jnp.concatenate([high, high, mid, mid, high, low], axis=axis)
    high, mid, low = right
    right = jnp.concatenate([high, mid, high, mid, low, high], axis=0)
    return lax.dot_general(
        left, right, (((axis,), (0,)), ((), ())), preferred_element_type=F32
    )


def eliminate(panel, pack, lower, work_ref, members):
    per_pack = LANES // PANEL
    start = panel * PANEL
    after = start + PANEL
    first = after // LANES * LANES
    total = work_ref.shape[2]
    owner = lax.broadcasted_iota(jnp.int32, (PANEL, LANES), 1) // PANEL
    spread = jnp.concatenate(
        [jnp.where(owner == place, lower, 0.0) for place in range(per_pack)], axis=0
    )
    stacked = jnp.concatenate(
        [
            work_ref[pack * per_pack + place, start:after, first:]
            for place in range(per_pack)
        ],
        axis=0,
    )
    solved = six_products(split3(spread), split3(stacked), 1)
    for place in range(per_pack):
        region = pack * per_pack + place
        rows = solved[place * PANEL : (place + 1) * PANEL]
        work_ref[region, start:after, members:] = rows[:, members - first :]
        if after < members:
            parts = split3(rows)
            change = six_products(
                [part[:, : members - first] for part in parts], parts, 0
            )
            work_ref[region, after:members, first:total] = (
                work_ref[region, after:members, first:total] - change[after - first :]
            )


def analysis_kernel(offsets, first_ref, prior_ref, column_ref, weight_ref, *rest):
    count = len(offsets)
    hbm_refs = rest[:count]
    out_ref, scaled_ref, work_ref, mean_ref, sems = rest[count : count + 5]
    vmem_refs = rest[count + 5 :]
    states_ref, obs_refs = vmem_refs[0], vmem_refs[1:]
    regions, members = prior_ref.shape
    sources, members_dev = states_ref.shape[0], states_ref.shape[2]
    points = states_ref.shape[3]
    packs = regions * PANEL // LANES
    ways = scaled_ref.shape[0]
    batches = sems.shape[0]
    batch_regions = regions // batches

    def loads(batch):
        copies = []
        for index, (hbm, vmem) in enumerate(zip(hbm_refs, vmem_refs)):
            size = vmem.shape[1] // batches
            copies.append(
                pltpu.make_async_copy(
                    hbm.at[:, pl.ds(offsets[index] + batch * size, size)],
                    vmem.at[:, pl.ds(batch * size, size)],
                    sems.at[batch, index],
                )
            )
        return copies

    for batch in range(batches):
        for copy in loads(batch):
            copy.start()

    @pl.loop(0, batches)
    def _(batch):
        for copy in loads(batch):
            copy.wait()

        @pl.loop(0, batch_regions // ways)
        def _(step):
            for way in range(ways):
                region_setup(
                    batch * batch_regions + step * ways + way, first_ref[0], prior_ref,
                    column_ref, weight_ref, states_ref, obs_refs, scaled_ref.at[way],
                    work_ref, mean_ref,
                )

    for panel in range(members // PANEL):
        lowers = factor_diagonals(panel, range(packs), work_ref)
        for pack in range(packs):
            eliminate(panel, pack, lowers[pack], work_ref, members)

    @pl.loop(0, regions)
    def _(region):
        moved = work_ref[region, :, members : members + points]
        solved = work_ref[region, :, members + points :]
        solved = jnp.concatenate([solved] * (points // LANES), axis=1)
        shift = mean_ref[region, :1] + jnp.sum(solved * moved, axis=0, keepdims=True)
        result = (shift + jnp.sqrt(members - 1.0) * moved).astype(BF16)
        for source in range(sources):
            out_ref[source, region] = result[
                source * members_dev : (source + 1) * members_dev
            ]


def analyse(first, prior_rows, weight_rows, states, obs_parts, slots):
    regions, members = prior_rows.shape
    sources, _, members_dev, points = states[0].shape
    width = obs_parts[0][0].shape[3]
    vmem = pl.BlockSpec(memory_space=pltpu.VMEM)
    loaded = [states] + obs_parts
    sizes = [regions] + [regions * slots] * len(obs_parts)
    columns = jnp.broadcast_to(prior_rows[:, :, None], (regions, members, LANES))
    return pl.pallas_call(
        functools.partial(analysis_kernel, [offset for _, offset in loaded]),
        out_shape=jax.ShapeDtypeStruct((sources, regions, members_dev, points), BF16),
        in_specs=[pl.BlockSpec(memory_space=pltpu.SMEM), vmem, vmem, vmem]
        + [pl.BlockSpec(memory_space=pl.ANY)] * len(loaded),
        out_specs=vmem,
        scratch_shapes=[
            pltpu.VMEM((2, members, slots * width), BF16),
            pltpu.VMEM((regions, members, members + points + LANES), F32),
            pltpu.VMEM((regions, 8, points), F32),
            pltpu.SemaphoreType.DMA((regions // 2, len(loaded))),
        ]
        + [
            pltpu.VMEM(array.shape[:1] + (size,) + array.shape[2:], array.dtype)
            for (array, _), size in zip(loaded, sizes)
        ],
        cost_estimate=pl.CostEstimate(
            flops=16 * regions * members * members * (slots * width + points),
            bytes_accessed=2 * regions * members * (slots * width + 2 * points),
            transcendentals=0,
        ),
        compiler_params=pltpu.CompilerParams(vmem_limit_bytes=48 << 20),
    )(first, prior_rows, columns, weight_rows, *[array for array, _ in loaded])


def body(
    ensemble_state, obs_ens, innovation, obs_prec, block_list, block_count, loc_weight, prior_weight
):
    spaces = lax.axis_size("space")
    mem_count = lax.axis_size("mem")
    members_dev, regions_dev, points = ensemble_state.shape
    blocks_dev, width = obs_ens.shape[1:]
    group_size = regions_dev // mem_count
    slots = block_list.shape[1]
    part = group_size // SPLIT
    first_row = lax.axis_index("mem") * group_size

    inner = 2 ** ((spaces.bit_length() - 1) // 2)
    cycle = grid_cycle(spaces // inner, inner)
    forward = [(cycle[k], cycle[(k + 1) % spaces]) for k in range(spaces)]
    backward = [(to, start) for start, to in forward]
    position = [cycle.index(space) for space in range(spaces)]
    half_way = spaces // 2

    def place_of(space):
        return sum(
            jnp.where(space == index, position[index], 0) for index in range(spaces)
        )

    all_ids = block_list.reshape(regions_dev * slots)
    behind = place_of(lax.axis_index("space")) - place_of(all_ids // blocks_dev)
    places = (behind + spaces) % spaces * blocks_dev + all_ids % blocks_dev
    active = jnp.arange(slots, dtype=jnp.int32)[None, :] < block_count[:, None]
    local = jnp.where(active, loc_weight, 0.0).reshape(regions_dev * slots)
    waiting = []
    start = 0
    for share in CHUNKS:
        stop = start + members_dev // share
        waiting.append(jnp.transpose(obs_ens[start:stop], (1, 0, 2)))
        start = stop
    rows = jnp.concatenate([obs_prec, innovation], axis=1)
    rows_ahead, rows_back = [rows], [rows]

    def ring_step(step, ahead, back):
        if step < half_way - 1:
            return lax.ppermute(ahead, "space", forward), lax.ppermute(
                back, "space", backward
            )
        middle = blocks_dev // 2
        return (
            lax.ppermute(ahead[:middle], "space", forward),
            lax.ppermute(back[middle:], "space", backward),
        )

    def exchange(picked):
        return lax.all_to_all(picked, "mem", split_axis=0, concat_axis=0, tiled=True)

    running = []
    obs_parts = [[] for _ in range(SPLIT)]
    stage = 0
    due = {}
    while waiting or running:
        if waiting and (not running or running[-1]["step"] == half_way - 1):
            own = waiting.pop(0)
            running.append({"step": 0, "ahead": [own], "back": [own]})
        moved = [
            ring_step(ring["step"], ring["ahead"][-1], ring["back"][-1])
            for ring in running
        ]
        tied = {"moved": moved, "waiting": waiting, "due": due.pop(stage, None)}
        if stage < half_way:
            tied["ahead"] = lax.ppermute(rows_ahead[-1], "space", forward)
        if stage < half_way - 1:
            tied["back"] = lax.ppermute(rows_back[-1], "space", backward)
        if stage == 0:
            tied["state"] = ensemble_state
        if stage == half_way - 1:
            tied["states"] = states
            tied["weights"] = weights(
                places, local, rows_ahead + [tied.pop("ahead")] + rows_back[:0:-1]
            )
        tied = lax.optimization_barrier(tied)
        waiting = tied["waiting"]
        for ring, (ahead, back) in zip(running, tied["moved"]):
            ring["ahead"].append(ahead)
            ring["back"].append(back)
            ring["step"] += 1
        if stage < half_way - 1:
            rows_ahead.append(tied["ahead"])
            rows_back.append(tied["back"])
        if stage == 0:
            by_region = jnp.transpose(tied["state"], (1, 0, 2)).reshape(
                mem_count, group_size, members_dev, points
            )
            states = exchange(by_region)
        if stage == half_way - 1:
            latest = states = tied["states"]
            weight_rows = tied["weights"]
        if running[0]["step"] == half_way:
            ring = running.pop(0)
            shards = ring["ahead"] + ring["back"][:0:-1]
            if waiting or running:
                picked = pick(
                    places, weight_rows, shards, mem_count, group_size, 0, group_size
                )
                due[stage + 1] = picked
                picked, _ = lax.optimization_barrier((picked, latest))
                latest = exchange(picked)
                due[stage + half_way - 1] = latest
                for index in range(SPLIT):
                    obs_parts[index].append((latest, index * part * slots))
            else:
                for index in range(SPLIT):
                    picked = pick(
                        places, weight_rows, shards, mem_count, group_size,
                        index * part, part,
                    )
                    picked, _ = lax.optimization_barrier((picked, latest))
                    latest = exchange(picked)
                    obs_parts[index].append((latest, 0))
        stage += 1

    results = []
    for index in range(SPLIT):
        start = first_row + index * part
        result = analyse(
            (start * slots).reshape(1),
            lax.dynamic_slice_in_dim(prior_weight, start, part, 0),
            weight_rows,
            (states, index * part),
            obs_parts[index],
            slots,
        )
        results.append(exchange(result))
    back = jnp.concatenate(results, axis=1)
    return jnp.transpose(back.reshape(regions_dev, members_dev, points), (1, 0, 2))


def solution(mesh):
    return jax.shard_map(
        body,
        mesh=mesh,
        in_specs=(
            P("mem", "space", None),
            P("mem", "space", None),
            P("space", None),
            P("space", None),
            P("space", None),
            P("space"),
            P("space", None),
            P("space", None),
        ),
        out_specs=P("mem", "space", None),
        check_vma=False,
    )
```

profile of v0, /device:TPU:0, one launch (start us, length us, event | category | flops | bytes accessed | tf_op | source)
XLA Modules:
  0.0 269.1 jit_solution(11510996505455786167)
XLA Ops:
  1.8 3.0 %collective-permute-start.2 = (bf16[64,32,128]{2,1,0:T(8,128)(2,1)S(1)}, bf16[64,32,128]{2,1,0:T(8,128)(2,1)S(1)}, u32[]{:S(2)}, u32[]{:S(2)}) collective-permute-start(bf16[64,32,128]{2,1,0:T(8,128)(2,1)S(1)} %bitcast.18), channel_id=1, source_target_pairs={{4,12},{12,20},{20,28},{28,24},{24,16},{16,8},{8,0},{0,4},{5,13},{... | collective-permute-start | bytes 1572872 | tf_op jit(solution)/shard_map/ppermute | solution.py:477
  5.0 1.9 collective-permute-start
  7.4 10.8 %collective-permute-done.rest_1_ = f32[64,256]{1,0:T(8,128)S(1)} collective-permute-done((f32[64,256]{1,0:T(8,128)S(1)}, f32[64,256]{1,0:T(8,128)S(1)}, u32[]{:S(2)}, u32[]{:S(2)}) %collective-permute-start) | collective-permute-done | bytes 65568 | tf_op jit(solution)/shard_map/ppermute | solution.py:503
  19.6 1.6 collective-permute-start.6
  21.7 2.5 copy.15
  24.2 4.6 %all-to-all-start = ((bf16[4,16,64,256]{3,2,1,0:T(8,128)(2,1)}), bf16[4,16,64,256]{3,2,1,0:T(8,128)(2,1)}, u32[]{:S(2)}, u32[]{:S(2)}) async-start(bf16[4,16,64,256]{3,2,1,0:T(8,128)(2,1)} %bitcast.21), calls=%async_computation | async-start | bytes 4194304 | tf_op jit(solution)/shard_map/all_to_all | solution.py:487
  30.9 2.6 collective-permute-done.4.rest_2_
  34.8 1.6 collective-permute-start.10
  40.5 9.2 %collective-permute-done.8.rest_3_ = f32[64,256]{1,0:T(8,128)S(1)} collective-permute-done((f32[64,256]{1,0:T(8,128)S(1)}, f32[64,256]{1,0:T(8,128)S(1)}, u32[]{:S(2)}, u32[]{:S(2)}) %collective-permute-start.8) | collective-permute-done | bytes 65568 | tf_op jit(solution)/shard_map/ppermute | solution.py:503
  49.8 2.1 collective-permute-done.9.rest_5_
  51.9 1.6 collective-permute-start.14
  57.6 1.6 collective-permute-start.16
  60.6 10.8 %collective-permute-done.16.rest_4_ = f32[64,256]{1,0:T(8,128)} collective-permute-done((f32[64,256]{1,0:T(8,128)S(1)}, f32[64,256]{1,0:T(8,128)}, u32[]{:S(2)}, u32[]{:S(2)}) %collective-permute-start.16) | collective-permute-done | bytes 65568 | tf_op jit(solution)/shard_map/ppermute | solution.py:503
  71.4 3.2 %shard_map.82.scale_ref.weight_ref = f32[512,256]{1,0:T(8,128)} custom-call(s32[512]{0:T(512)} %fusion.3.ids_ref, f32[512]{0:T(512)} %reshape.24.local_ref, f32[64,256]{1,0:T(8,128)} %copy-done.23, f32[64,256]{1,0:T(8,128)} %copy-done.24, f32[64,256]{1,0:T(8,128)} %copy-done.26, f32[64,256]{1,0:T(8,128)} %copy-done.28, ...), custom_call_target="tpu_custom_call" | custom-call | tf_op jit(solution)/shard_map/pallas_call | solution.py:54
  80.5 2.4 shard_map.83
  83.0 2.0 copy-done
  85.0 5.0 %all-to-all-start.1 = ((bf16[4,128,32,128]{3,2,1,0:T(8,128)(2,1)}), bf16[4,128,32,128]{3,2,1,0:T(8,128)(2,1)}, u32[]{:S(2)}, u32[]{:S(2)}) async-start(bf16[4,128,32,128]{3,2,1,0:T(8,128)(2,1)} %copy-done), calls=%async_computation.1 | async-start | bytes 8388608 | tf_op jit(solution)/shard_map/all_to_all | solution.py:487
  90.0 1.6 collective-permute-start.17
  92.1 12.2 %collective-permute-done.17.rest_2_ = bf16[64,32,128]{2,1,0:T(8,128)(2,1)S(1)} collective-permute-done((bf16[64,32,128]{2,1,0:T(8,128)(2,1)S(1)}, bf16[64,32,128]{2,1,0:T(8,128)(2,1)S(1)}, u32[]{:S(2)}, u32[]{:S(2)}) %collective-permute-start.17) | collective-permute-done | bytes 524320 | tf_op jit(solution)/shard_map/ppermute | solution.py:477
  109.2 9.6 %collective-permute-done.19.rest_3_ = bf16[64,32,128]{2,1,0:T(8,128)(2,1)S(1)} collective-permute-done((bf16[64,32,128]{2,1,0:T(8,128)(2,1)S(1)}, bf16[64,32,128]{2,1,0:T(8,128)(2,1)S(1)}, u32[]{:S(2)}, u32[]{:S(2)}) %collective-permute-start.19) | collective-permute-done | bytes 524320 | tf_op jit(solution)/shard_map/ppermute | solution.py:477
  122.3 4.4 %collective-permute-done.21.rest_4_ = bf16[32,32,128]{2,1,0:T(8,128)(2,1)S(1)} collective-permute-done((bf16[32,32,128]{2,1,0:T(8,128)(2,1)S(1)}, bf16[32,32,128]{2,1,0:T(8,128)(2,1)S(1)}, u32[]{:S(2)}, u32[]{:S(2)}) %collective-permute-start.21) | collective-permute-done | bytes 262176 | tf_op jit(solution)/shard_map/ppermute | solution.py:482
  128.1 10.1 %all-to-all-done.1.rest_1_ = bf16[4,128,32,128]{3,2,1,0:T(8,128)(2,1)} async-done(((bf16[4,128,32,128]{3,2,1,0:T(8,128)(2,1)}), bf16[4,128,32,128]{3,2,1,0:T(8,128)(2,1)}, u32[]{:S(2)}, u32[]{:S(2)}) %all-to-all-start.1) | async-done | bytes 4194336 | tf_op jit(solution)/shard_map/all_to_all | solution.py:487
  141.3 2.8 %shard_map.84 = bf16[4,64,32,128]{3,2,1,0:T(8,128)(2,1)} custom-call(s32[512]{0:T(512)S(1)} %copy-done.21, f32[512,256]{1,0:T(8,128)S(1)} %copy-done.2, bf16[64,32,128]{2,1,0:T(8,128)(2,1)S(1)} %bitcast.16, bf16[64,32,128]{2,1,0:T(8,128)(2,1)S(1)} %collective-permute-done.14.rest_1_, bf16[64,32,128]{2,1,0:T(8,128)(2,1)S(1)} %copy-done.4, ...), custom_call_target="tpu_custom_call" | custom-call | flops 1048576 | bytes 12582912 | tf_op jit(solution)/shard_map/pallas_call | solution.py:94
  144.1 4.5 %all-to-all-start.2 = ((bf16[4,64,32,128]{3,2,1,0:T(8,128)(2,1)}), bf16[4,64,32,128]{3,2,1,0:T(8,128)(2,1)}, u32[]{:S(2)}, u32[]{:S(2)}) async-start(bf16[4,64,32,128]{3,2,1,0:T(8,128)(2,1)} %shard_map.84), calls=%async_computation.2 | async-start | bytes 4194304 | tf_op jit(solution)/shard_map/all_to_all | solution.py:487
  151.6 2.8 %shard_map.86 = bf16[4,64,32,128]{3,2,1,0:T(8,128)(2,1)} custom-call(s32[512]{0:T(512)S(1)} %copy-done.21, f32[512,256]{1,0:T(8,128)S(1)} %copy-done.2, bf16[64,32,128]{2,1,0:T(8,128)(2,1)S(1)} %bitcast.17, bf16[64,32,128]{2,1,0:T(8,128)(2,1)S(1)} %collective-permute-done.14.rest_1_, bf16[64,32,128]{2,1,0:T(8,128)(2,1)S(1)} %copy-done.5, ...), custom_call_target="tpu_custom_call" | custom-call | flops 1048576 | bytes 12582912 | tf_op jit(solution)/shard_map/pallas_call | solution.py:94
  154.3 20.0 %all-to-all-done.2.rest_2_ = bf16[4,64,32,128]{3,2,1,0:T(8,128)(2,1)} async-done(((bf16[4,64,32,128]{3,2,1,0:T(8,128)(2,1)}), bf16[4,64,32,128]{3,2,1,0:T(8,128)(2,1)}, u32[]{:S(2)}, u32[]{:S(2)}) %all-to-all-start.2) | async-done | bytes 2097184 | tf_op jit(solution)/shard_map/all_to_all | solution.py:487
  174.3 4.4 %all-to-all-start.4 = ((bf16[4,64,32,128]{3,2,1,0:T(8,128)(2,1)}), bf16[4,64,32,128]{3,2,1,0:T(8,128)(2,1)}, u32[]{:S(2)}, u32[]{:S(2)}) async-start(bf16[4,64,32,128]{3,2,1,0:T(8,128)(2,1)} %shard_map.86), calls=%async_computation.4 | async-start | bytes 4194304 | tf_op jit(solution)/shard_map/all_to_all | solution.py:487
  179.8 28.2 %shard_map.85 = bf16[4,8,64,256]{3,2,1,0:T(8,128)(2,1)} custom-call(s32[1]{0:T(128)} %bitcast.first_ref, f32[8,256]{1,0:T(8,128)S(1)} %get-tuple-element.69.prior_ref, f32[8,256,128]{2,1,0:T(8,128)S(1)} %broadcast_in_dim.40.column_ref, f32[512,256]{1,0:T(8,128)S(1)} %copy-done.2, bf16[4,16,64,256]{3,2,1,0:T(8,128)(2,1)} %all-to-all-done.rest_0_, ...), custom_call_target="tpu_custom_call" | custom-call | flops 10737418240 | bytes 6291456 | tf_op jit(solution)/shard_map/pallas_call | solution.py:412
  208.0 3.5 %all-to-all-start.3 = ((bf16[4,8,64,256]{3,2,1,0:T(8,128)(2,1)}), bf16[4,8,64,256]{3,2,1,0:T(8,128)(2,1)S(1)}, u32[]{:S(2)}, u32[]{:S(2)}) async-start(bf16[4,8,64,256]{3,2,1,0:T(8,128)(2,1)} %shard_map.85), calls=%async_computation.3 | async-start | bytes 2097152 | tf_op jit(solution)/shard_map/all_to_all | solution.py:487
  211.9 36.8 %shard_map.87 = bf16[4,8,64,256]{3,2,1,0:T(8,128)(2,1)S(1)} custom-call(s32[1]{0:T(128)} %bitcast.5.first_ref, f32[8,256]{1,0:T(8,128)S(1)} %get-tuple-element.70.prior_ref, f32[8,256,128]{2,1,0:T(8,128)S(1)} %broadcast_in_dim.44.column_ref, f32[512,256]{1,0:T(8,128)S(1)} %copy-done.2, bf16[4,16,64,256]{3,2,1,0:T(8,128)(2,1)} %all-to-all-done.rest_0_, ...), custom_call_target="tpu_custom_call" | custom-call | flops 10737418240 | bytes 6291456 | tf_op jit(solution)/shard_map/pallas_call | solution.py:412
  248.7 17.5 %all_to_all.30 = bf16[4,8,64,256]{3,2,1,0:T(8,128)(2,1)S(1)} all-to-all(bf16[4,8,64,256]{3,2,1,0:T(8,128)(2,1)S(1)} %shard_map.87), channel_id=1, replica_groups=mesh['space'=8,'mem'=4] {'mem'}, dimensions={0} | all-to-all | bytes 2097152 | tf_op jit(solution)/shard_map/all_to_all | solution.py:487
  266.4 2.5 copy.24
  (122 shorter events, 40.8 us)
Async XLA Ops:
  1.8 17.8 %collective-permute-start.2 = (bf16[64,32,128]{2,1,0:T(8,128)(2,1)S(1)}, bf16[64,32,128]{2,1,0:T(8,128)(2,1)S(1)}, u32[]{:S(2)}, u32[]{:S(2)}) collective-permute-start(bf16[64,32,128]{2,1,0:T(8,128)(2,1)S(1)} %bitcast.18), channel_id=1, source_target_pairs={{4,12},{12,20},{20,28},{28,24},{24,16},{16,8},{8,0},{0,4},{5,13},{... | collective-permute-start | bytes 1572872 | tf_op jit(solution)/shard_map/ppermute | solution.py:477
  4.8 14.8 %collective-permute-start.3 = (bf16[64,32,128]{2,1,0:T(8,128)(2,1)S(1)}, bf16[64,32,128]{2,1,0:T(8,128)(2,1)S(1)}, u32[]{:S(2)}, u32[]{:S(2)}) collective-permute-start(bf16[64,32,128]{2,1,0:T(8,128)(2,1)S(1)} %bitcast.19), channel_id=1, source_target_pairs={{12,4},{20,12},{28,20},{24,28},{16,24},{8,16},{0,8},{4,0},{13,5},{... | collective-permute-start | bytes 1572872 | tf_op jit(solution)/shard_map/ppermute | solution.py:477
  5.0 13.2 %collective-permute-start = (f32[64,256]{1,0:T(8,128)S(1)}, f32[64,256]{1,0:T(8,128)S(1)}, u32[]{:S(2)}, u32[]{:S(2)}) collective-permute-start(f32[64,256]{1,0:T(8,128)S(1)} %constant_dynamic-update-slice_fusion.rest_0_), channel_id=1, source_target_pairs={{4,12},{12,20},{20,28},{28,24},{24,16},{16,8},{8,0},{0,4},{5,13},{... | collective-permute-start | bytes 196616 | tf_op jit(solution)/shard_map/ppermute | solution.py:503
  6.9 12.7 %collective-permute-start.1 = (f32[64,256]{1,0:T(8,128)S(1)}, f32[64,256]{1,0:T(8,128)S(1)}, u32[]{:S(2)}, u32[]{:S(2)}) collective-permute-start(f32[64,256]{1,0:T(8,128)S(1)} %constant_dynamic-update-slice_fusion.rest_0_), channel_id=1, source_target_pairs={{12,4},{20,12},{28,20},{24,28},{16,24},{8,16},{0,8},{4,0},{13,5},{... | collective-permute-start | bytes 196616 | tf_op jit(solution)/shard_map/ppermute | solution.py:505
  19.6 15.2 %collective-permute-start.6 = (bf16[64,32,128]{2,1,0:T(8,128)(2,1)S(1)}, bf16[64,32,128]{2,1,0:T(8,128)(2,1)S(1)}, u32[]{:S(2)}, u32[]{:S(2)}) collective-permute-start(bf16[64,32,128]{2,1,0:T(8,128)(2,1)S(1)} %collective-permute-done.2.rest_1_), channel_id=1, source_target_pairs={{4,12},{12,20},{20,28},{28,24},{24,16},{16,8},{8,0},{0,4},{5,13},{... | collective-permute-start | bytes 1572872 | tf_op jit(solution)/shard_map/ppermute | solution.py:477
  21.2 13.6 %collective-permute-start.7 = (bf16[64,32,128]{2,1,0:T(8,128)(2,1)S(1)}, bf16[64,32,128]{2,1,0:T(8,128)(2,1)S(1)}, u32[]{:S(2)}, u32[]{:S(2)}) collective-permute-start(bf16[64,32,128]{2,1,0:T(8,128)(2,1)S(1)} %collective-permute-done.3.rest_8_), channel_id=1, source_target_pairs={{12,4},{20,12},{28,20},{24,28},{16,24},{8,16},{0,8},{4,0},{13,5},{... | collective-permute-start | bytes 1572872 | tf_op jit(solution)/shard_map/ppermute | solution.py:477
  24.2 33.2 %copy-start.33 = (f32[64,8]{0,1:T(8,128)S(1)}, f32[64,8]{0,1:T(8,128)}, u32[]{:S(2)}) copy-start(f32[64,8]{0,1:T(8,128)} %param.14) | copy-start | bytes 6148
  24.2 33.2 %copy-start.32 = (s32[64,8]{0,1:T(8,128)S(1)}, s32[64,8]{0,1:T(8,128)}, u32[]{:S(2)}) copy-start(s32[64,8]{0,1:T(8,128)} %param.12) | copy-start | bytes 6148
  24.2 50.4 %all-to-all-start = ((bf16[4,16,64,256]{3,2,1,0:T(8,128)(2,1)}), bf16[4,16,64,256]{3,2,1,0:T(8,128)(2,1)}, u32[]{:S(2)}, u32[]{:S(2)}) async-start(bf16[4,16,64,256]{3,2,1,0:T(8,128)(2,1)} %bitcast.21), calls=%async_computation | async-start | bytes 4194304 | tf_op jit(solution)/shard_map/all_to_all | solution.py:487
  28.8 4.7 %collective-permute-start.4 = (f32[64,256]{1,0:T(8,128)S(1)}, f32[64,256]{1,0:T(8,128)S(1)}, u32[]{:S(2)}, u32[]{:S(2)}) collective-permute-start(f32[64,256]{1,0:T(8,128)S(1)} %collective-permute-done.rest_1_), channel_id=1, source_target_pairs={{4,12},{12,20},{20,28},{28,24},{24,16},{16,8},{8,0},{0,4},{5,13},{... | collective-permute-start | bytes 196616 | tf_op jit(solution)/shard_map/ppermute | solution.py:503
  30.4 4.4 %collective-permute-start.5 = (f32[64,256]{1,0:T(8,128)S(1)}, f32[64,256]{1,0:T(8,128)S(1)}, u32[]{:S(2)}, u32[]{:S(2)}) collective-permute-start(f32[64,256]{1,0:T(8,128)S(1)} %collective-permute-done.1.rest_7_), channel_id=1, source_target_pairs={{12,4},{20,12},{28,20},{24,28},{16,24},{8,16},{0,8},{4,0},{13,5},{... | collective-permute-start | bytes 196616 | tf_op jit(solution)/shard_map/ppermute | solution.py:505
  34.8 17.0 %collective-permute-start.10 = (bf16[64,32,128]{2,1,0:T(8,128)(2,1)S(1)}, bf16[64,32,128]{2,1,0:T(8,128)(2,1)S(1)}, u32[]{:S(2)}, u32[]{:S(2)}) collective-permute-start(bf16[64,32,128]{2,1,0:T(8,128)(2,1)S(1)} %collective-permute-done.6.rest_2_), channel_id=1, source_target_pairs={{4,12},{12,20},{20,28},{28,24},{24,16},{16,8},{8,0},{0,4},{5,13},{... | collective-permute-start | bytes 1572872 | tf_op jit(solution)/shard_map/ppermute | solution.py:477
  37.2 14.6 %collective-permute-start.11 = (bf16[64,32,128]{2,1,0:T(8,128)(2,1)S(1)}, bf16[64,32,128]{2,1,0:T(8,128)(2,1)S(1)}, u32[]{:S(2)}, u32[]{:S(2)}) collective-permute-start(bf16[64,32,128]{2,1,0:T(8,128)(2,1)S(1)} %collective-permute-done.7.rest_7_), channel_id=1, source_target_pairs={{12,4},{20,12},{28,20},{24,28},{16,24},{8,16},{0,8},{4,0},{13,5},{... | collective-permute-start | bytes 1572872 | tf_op jit(solution)/shard_map/ppermute | solution.py:477
  38.5 11.3 %collective-permute-start.8 = (f32[64,256]{1,0:T(8,128)S(1)}, f32[64,256]{1,0:T(8,128)S(1)}, u32[]{:S(2)}, u32[]{:S(2)}) collective-permute-start(f32[64,256]{1,0:T(8,128)S(1)} %collective-permute-done.4.rest_2_), channel_id=1, source_target_pairs={{4,12},{12,20},{20,28},{28,24},{24,16},{16,8},{8,0},{0,4},{5,13},{... | collective-permute-start | bytes 196616 | tf_op jit(solution)/shard_map/ppermute | solution.py:503
  40.1 11.8 %collective-permute-start.9 = (f32[64,256]{1,0:T(8,128)S(1)}, f32[64,256]{1,0:T(8,128)S(1)}, u32[]{:S(2)}, u32[]{:S(2)}) collective-permute-start(f32[64,256]{1,0:T(8,128)S(1)} %collective-permute-done.5.rest_6_), channel_id=1, source_target_pairs={{12,4},{20,12},{28,20},{24,28},{16,24},{8,16},{0,8},{4,0},{13,5},{... | collective-permute-start | bytes 196616 | tf_op jit(solution)/shard_map/ppermute | solution.py:505
  51.9 22.8 %collective-permute-start.14 = (bf16[64,32,128]{2,1,0:T(8,128)(2,1)S(1)}, bf16[64,32,128]{2,1,0:T(8,128)(2,1)S(1)}, u32[]{:S(2)}, u32[]{:S(2)}) collective-permute-start(bf16[64,32,128]{2,1,0:T(8,128)(2,1)S(1)} %bitcast.14), channel_id=1, source_target_pairs={{4,12},{12,20},{20,28},{28,24},{24,16},{16,8},{8,0},{0,4},{5,13},{... | collective-permute-start | bytes 1572872 | tf_op jit(solution)/shard_map/ppermute | solution.py:477
  53.5 21.1 %collective-permute-start.15 = (bf16[64,32,128]{2,1,0:T(8,128)(2,1)S(1)}, bf16[64,32,128]{2,1,0:T(8,128)(2,1)S(1)}, u32[]{:S(2)}, u32[]{:S(2)}) collective-permute-start(bf16[64,32,128]{2,1,0:T(8,128)(2,1)S(1)} %bitcast.15), channel_id=1, source_target_pairs={{12,4},{20,12},{28,20},{24,28},{16,24},{8,16},{0,8},{4,0},{13,5},{... | collective-permute-start | bytes 1572872 | tf_op jit(solution)/shard_map/ppermute | solution.py:477
  54.6 20.0 %collective-permute-start.12 = (bf16[32,32,128]{2,1,0:T(8,128)(2,1)}, bf16[32,32,128]{2,1,0:T(8,128)(2,1)S(1)}, u32[]{:S(2)}, u32[]{:S(2)}) collective-permute-start(bf16[32,32,128]{2,1,0:T(8,128)(2,1)} %slice.20), channel_id=1, source_target_pairs={{4,12},{12,20},{20,28},{28,24},{24,16},{16,8},{8,0},{0,4},{5,13},{... | collective-permute-start | bytes 786440 | tf_op jit(solution)/shard_map/ppermute | solution.py:482
  56.9 17.7 %collective-permute-start.13 = (bf16[32,32,128]{2,1,0:T(8,128)(2,1)}, bf16[32,32,128]{2,1,0:T(8,128)(2,1)}, u32[]{:S(2)}, u32[]{:S(2)}) collective-permute-start(bf16[32,32,128]{2,1,0:T(8,128)(2,1)} %slice.21), channel_id=1, source_target_pairs={{12,4},{20,12},{28,20},{24,28},{16,24},{8,16},{0,8},{4,0},{13,5},{... | collective-permute-start | bytes 786440 | tf_op jit(solution)/shard_map/ppermute | solution.py:483
  57.6 13.8 %collective-permute-start.16 = (f32[64,256]{1,0:T(8,128)S(1)}, f32[64,256]{1,0:T(8,128)}, u32[]{:S(2)}, u32[]{:S(2)}) collective-permute-start(f32[64,256]{1,0:T(8,128)S(1)} %collective-permute-done.8.rest_3_), channel_id=1, source_target_pairs={{4,12},{12,20},{20,28},{28,24},{24,16},{16,8},{8,0},{0,4},{5,13},{... | collective-permute-start | bytes 196616 | tf_op jit(solution)/shard_map/ppermute | solution.py:503
  84.9 53.3 %copy-start.2 = (f32[512,256]{1,0:T(8,128)S(1)}, f32[512,256]{1,0:T(8,128)}, u32[]{:S(2)}) copy-start(f32[512,256]{1,0:T(8,128)} %shard_map.82.scale_ref.weight_ref) | copy-start | bytes 1572868
  84.9 53.3 %copy-start.21 = (s32[512]{0:T(512)S(1)}, s32[512]{0:T(512)}, u32[]{:S(2)}) copy-start(s32[512]{0:T(512)} %fusion.3.ids_ref) | copy-start | bytes 6148
  85.0 53.3 %all-to-all-start.1 = ((bf16[4,128,32,128]{3,2,1,0:T(8,128)(2,1)}), bf16[4,128,32,128]{3,2,1,0:T(8,128)(2,1)}, u32[]{:S(2)}, u32[]{:S(2)}) async-start(bf16[4,128,32,128]{3,2,1,0:T(8,128)(2,1)} %copy-done), calls=%async_computation.1 | async-start | bytes 8388608 | tf_op jit(solution)/shard_map/all_to_all | solution.py:487
  90.0 14.3 %collective-permute-start.17 = (bf16[64,32,128]{2,1,0:T(8,128)(2,1)S(1)}, bf16[64,32,128]{2,1,0:T(8,128)(2,1)S(1)}, u32[]{:S(2)}, u32[]{:S(2)}) collective-permute-start(bf16[64,32,128]{2,1,0:T(8,128)(2,1)S(1)} %collective-permute-done.14.rest_1_), channel_id=1, source_target_pairs={{4,12},{12,20},{20,28},{28,24},{24,16},{16,8},{8,0},{0,4},{5,13},{... | collective-permute-start | bytes 1572872 | tf_op jit(solution)/shard_map/ppermute | solution.py:477
  91.6 14.0 %collective-permute-start.18 = (bf16[64,32,128]{2,1,0:T(8,128)(2,1)S(1)}, bf16[64,32,128]{2,1,0:T(8,128)(2,1)S(1)}, u32[]{:S(2)}, u32[]{:S(2)}) collective-permute-start(bf16[64,32,128]{2,1,0:T(8,128)(2,1)S(1)} %collective-permute-done.15.rest_8_), channel_id=1, source_target_pairs={{12,4},{20,12},{28,20},{24,28},{16,24},{8,16},{0,8},{4,0},{13,5},{... | collective-permute-start | bytes 1572872 | tf_op jit(solution)/shard_map/ppermute | solution.py:477
  105.6 13.3 %collective-permute-start.19 = (bf16[64,32,128]{2,1,0:T(8,128)(2,1)S(1)}, bf16[64,32,128]{2,1,0:T(8,128)(2,1)S(1)}, u32[]{:S(2)}, u32[]{:S(2)}) collective-permute-start(bf16[64,32,128]{2,1,0:T(8,128)(2,1)S(1)} %collective-permute-done.17.rest_2_), channel_id=1, source_target_pairs={{4,12},{12,20},{20,28},{28,24},{24,16},{16,8},{8,0},{0,4},{5,13},{... | collective-permute-start | bytes 1572872 | tf_op jit(solution)/shard_map/ppermute | solution.py:477
  107.2 13.0 %collective-permute-start.20 = (bf16[64,32,128]{2,1,0:T(8,128)(2,1)S(1)}, bf16[64,32,128]{2,1,0:T(8,128)(2,1)S(1)}, u32[]{:S(2)}, u32[]{:S(2)}) collective-permute-start(bf16[64,32,128]{2,1,0:T(8,128)(2,1)S(1)} %collective-permute-done.18.rest_7_), channel_id=1, source_target_pairs={{12,4},{20,12},{28,20},{24,28},{16,24},{8,16},{0,8},{4,0},{13,5},{... | collective-permute-start | bytes 1572872 | tf_op jit(solution)/shard_map/ppermute | solution.py:477
  120.2 6.6 %collective-permute-start.21 = (bf16[32,32,128]{2,1,0:T(8,128)(2,1)S(1)}, bf16[32,32,128]{2,1,0:T(8,128)(2,1)S(1)}, u32[]{:S(2)}, u32[]{:S(2)}) collective-permute-start(bf16[32,32,128]{2,1,0:T(8,128)(2,1)S(1)} %slice.22), channel_id=1, source_target_pairs={{4,12},{12,20},{20,28},{28,24},{24,16},{16,8},{8,0},{0,4},{5,13},{... | collective-permute-start | bytes 786440 | tf_op jit(solution)/shard_map/ppermute | solution.py:482
  121.0 6.4 %collective-permute-start.22 = (bf16[32,32,128]{2,1,0:T(8,128)(2,1)S(1)}, bf16[32,32,128]{2,1,0:T(8,128)(2,1)S(1)}, u32[]{:S(2)}, u32[]{:S(2)}) collective-permute-start(bf16[32,32,128]{2,1,0:T(8,128)(2,1)S(1)} %slice.23), channel_id=1, source_target_pairs={{12,4},{20,12},{28,20},{24,28},{16,24},{8,16},{0,8},{4,0},{13,5},{... | collective-permute-start | bytes 786440 | tf_op jit(solution)/shard_map/ppermute | solution.py:483
  144.1 30.2 %all-to-all-start.2 = ((bf16[4,64,32,128]{3,2,1,0:T(8,128)(2,1)}), bf16[4,64,32,128]{3,2,1,0:T(8,128)(2,1)}, u32[]{:S(2)}, u32[]{:S(2)}) async-start(bf16[4,64,32,128]{3,2,1,0:T(8,128)(2,1)} %shard_map.84), calls=%async_computation.2 | async-start | bytes 4194304 | tf_op jit(solution)/shard_map/all_to_all | solution.py:487
  174.3 33.7 %all-to-all-start.4 = ((bf16[4,64,32,128]{3,2,1,0:T(8,128)(2,1)}), bf16[4,64,32,128]{3,2,1,0:T(8,128)(2,1)}, u32[]{:S(2)}, u32[]{:S(2)}) async-start(bf16[4,64,32,128]{3,2,1,0:T(8,128)(2,1)} %shard_map.86), calls=%async_computation.4 | async-start | bytes 4194304 | tf_op jit(solution)/shard_map/all_to_all | solution.py:487
  208.0 40.7 %all-to-all-start.3 = ((bf16[4,8,64,256]{3,2,1,0:T(8,128)(2,1)}), bf16[4,8,64,256]{3,2,1,0:T(8,128)(2,1)S(1)}, u32[]{:S(2)}, u32[]{:S(2)}) async-start(bf16[4,8,64,256]{3,2,1,0:T(8,128)(2,1)} %shard_map.85), calls=%async_computation.3 | async-start | bytes 2097152 | tf_op jit(solution)/shard_map/all_to_all | solution.py:487
  (31 other events, 195.8 us)
where the time goes:
time: 272 us; the launch traced here: 269 us
  waiting for transfers between devices  97.8 us (36%)
  Pallas kernels  76.2 us (28%)
  starting transfers between devices  47.5 us (17%)
  local copies, waits for them, and re-layouts  28.8 us (11%)
  blocking collectives  17.5 us (6%)
    pallas_call x2, Pallas kernels, analyse(): pl.pallas_call(functools.partial(analysis_kernel, [offset for _, offset i...  65 us
    ppermute x4, waiting for transfers between devices, body(): tied['ahead'] = lax.ppermute(rows_ahead[-1], 'space', forward)  33.4 us
    all_to_all x5, waiting for transfers between devices, exchange(): lax.all_to_all(picked, 'mem', split_axis=0, concat_axis=0, tiled=True)  30.1 us
    all_to_all x5, starting transfers between devices, exchange(): lax.all_to_all(picked, 'mem', split_axis=0, concat_axis=0, tiled=True)  22 us
    ppermute x6, waiting for transfers between devices, ring_step(): lax.ppermute(ahead, 'space', forward)  21.9 us
    unnamed x74, local copies, waits for them, and re-layouts  18.6 us
    all_to_all x1, blocking collectives, exchange(): lax.all_to_all(picked, 'mem', split_axis=0, concat_axis=0, tiled=True)  17.5 us
    ppermute x6, starting transfers between devices, ring_step(): lax.ppermute(ahead, 'space', forward)  10.3 us
  transfers between devices with their start and end apart: 28, of which 15 were waited for; matrix products, arithmetic and copies ran while one was open for 3% of the time, Pallas kernels for 26%

commit v1 on v0

--- a/solution.py
+++ b/solution.py
@@ -9,7 +9,7 @@
 
 INFLATION = 1.1
 PANEL = 32
-GROUP = 4
+GROUP = 8
 LANES = 128
 CHUNKS = (2, 2)
 SPLIT = 2
@@ -128,7 +128,7 @@
 
 def region_setup(
     region, first, prior_ref, column_ref, weight_ref, states_ref, obs_refs, scaled_ref,
-    work_ref, mean_ref,
+    work_ref, lead_ref, mean_ref,
 ):
     members = prior_ref.shape[1]
     sources, members_dev = states_ref.shape[0], states_ref.shape[2]
@@ -176,7 +176,9 @@
     vector = root_col * (
         projection - jnp.sum(share_col * projection, axis=0, keepdims=True)
     )
-    work_ref[region, :, members + points :] = vector
+    lead_ref[region] = vector[:PANEL]
+    carried = lax.broadcasted_iota(jnp.int32, (members, LANES), 1) < PANEL
+    carried &= lax.broadcasted_iota(jnp.int32, (members, LANES), 0) >= PANEL
     for start in range(0, members, LANES):
         tile = slice(start, start + LANES)
         part = gram[:, tile]
@@ -185,9 +187,10 @@
         on_diag = lax.broadcasted_iota(jnp.int32, (members, LANES), 0) == (
             lax.broadcasted_iota(jnp.int32, (members, LANES), 1) + start
         )
-        work_ref[region, :, tile] = system + jnp.where(
-            on_diag, (members - 1) / INFLATION, 0.0
-        )
+        system = system + jnp.where(on_diag, (members - 1) / INFLATION, 0.0)
+        if start == 0:
+            system = jnp.where(carried, vector, system)
+        work_ref[region, :, tile] = system
     for start in range(0, points, LANES):
         states = jnp.concatenate(
             [
@@ -306,43 +309,56 @@
     )
 
 
-def eliminate(panel, pack, lower, work_ref, members):
+def eliminate(panel, pack, lower, work_ref, lead_ref, members):
     per_pack = LANES // PANEL
     start = panel * PANEL
     after = start + PANEL
-    first = after // LANES * LANES
-    total = work_ref.shape[2]
+    first = start // LANES * LANES
+    kept = after // LANES * LANES
     owner = lax.broadcasted_iota(jnp.int32, (PANEL, LANES), 1) // PANEL
+
+    def carry(region, rows, block):
+        if start % LANES:
+            return block
+        if start == 0:
+            source = lead_ref[region]
+        else:
+            source = work_ref[region, rows, first - LANES : first]
+        lane = lax.broadcasted_iota(jnp.int32, source.shape, 1)
+        head = jnp.where(lane < PANEL, source, block[:, :LANES])
+        return jnp.concatenate([head, block[:, LANES:]], axis=1)
+
     spread = jnp.concatenate(
         [jnp.where(owner == place, lower, 0.0) for place in range(per_pack)], axis=0
     )
-    stacked = jnp.concatenate(
-        [
-            work_ref[pack * per_pack + place, start:after, first:]
-            for place in range(per_pack)
-        ],
-        axis=0,
-    )
+    here, rest = slice(start, after), slice(after, members)
+    stacked = []
+    for place in range(per_pack):
+        region = pack * per_pack + place
+        stacked.append(carry(region, here, work_ref[region, here, first:]))
+    stacked = jnp.concatenate(stacked, axis=0)
     solved = six_products(split3(spread), split3(stacked), 1)
     for place in range(per_pack):
         region = pack * per_pack + place
         rows = solved[place * PANEL : (place + 1) * PANEL]
-        work_ref[region, start:after, members:] = rows[:, members - first :]
+        work_ref[region, here, first : first + LANES] = rows[:, :LANES]
+        work_ref[region, here, members:] = rows[:, members - first :]
         if after < members:
             parts = split3(rows)
             change = six_products(
-                [part[:, : members - first] for part in parts], parts, 0
+                [part[:, kept - first : members - first] for part in parts], parts, 0
             )
-            work_ref[region, after:members, first:total] = (
-                work_ref[region, after:members, first:total] - change[after - first :]
-            )
+            old = work_ref[region, rest, first:]
+            if start:
+                old = carry(region, rest, old)
+            work_ref[region, rest, first:] = old - change[after - kept :]
 
 
 def analysis_kernel(offsets, first_ref, prior_ref, column_ref, weight_ref, *rest):
     count = len(offsets)
     hbm_refs = rest[:count]
-    out_ref, scaled_ref, work_ref, mean_ref, sems = rest[count : count + 5]
-    vmem_refs = rest[count + 5 :]
+    out_ref, scaled_ref, work_ref, lead_ref, mean_ref, sems = rest[count : count + 6]
+    vmem_refs = rest[count + 6 :]
     states_ref, obs_refs = vmem_refs[0], vmem_refs[1:]
     regions, members = prior_ref.shape
     sources, members_dev = states_ref.shape[0], states_ref.shape[2]
@@ -380,19 +396,24 @@
                 region_setup(
                     batch * batch_regions + step * ways + way, first_ref[0], prior_ref,
                     column_ref, weight_ref, states_ref, obs_refs, scaled_ref.at[way],
-                    work_ref, mean_ref,
+                    work_ref, lead_ref, mean_ref,
                 )
 
     for panel in range(members // PANEL):
         lowers = factor_diagonals(panel, range(packs), work_ref)
         for pack in range(packs):
-            eliminate(panel, pack, lowers[pack], work_ref, members)
+            eliminate(panel, pack, lowers[pack], work_ref, lead_ref, members)
 
     @pl.loop(0, regions)
     def _(region):
         moved = work_ref[region, :, members : members + points]
-        solved = work_ref[region, :, members + points :]
-        solved = jnp.concatenate([solved] * (points // LANES), axis=1)
+        solved = jnp.concatenate(
+            [
+                work_ref[region, start : start + LANES, start : start + 1]
+                for start in range(0, members, LANES)
+            ],
+            axis=0,
+        )
         shift = mean_ref[region, :1] + jnp.sum(solved * moved, axis=0, keepdims=True)
         result = (shift + jnp.sqrt(members - 1.0) * moved).astype(BF16)
         for source in range(sources):
@@ -417,7 +438,8 @@
         out_specs=vmem,
         scratch_shapes=[
             pltpu.VMEM((2, members, slots * width), BF16),
-            pltpu.VMEM((regions, members, members + points + LANES), F32),
+            pltpu.VMEM((regions, members, members + points), F32),
+            pltpu.VMEM((regions, PANEL, LANES), F32),
             pltpu.VMEM((regions, 8, points), F32),
             pltpu.SemaphoreType.DMA((regions // 2, len(loaded))),
         ]
@@ -527,6 +549,11 @@
         if stage == half_way - 1:
             latest = states = tied["states"]
             weight_rows = tied["weights"]
+        if tied["due"] is not None:
+            picked, _ = lax.optimization_barrier((tied["due"], latest))
+            latest = exchange(picked)
+            for index in range(SPLIT):
+                obs_parts[index].append((latest, index * part * slots))
         if running[0]["step"] == half_way:
             ring = running.pop(0)
             shards = ring["ahead"] + ring["back"][:0:-1]
@@ -535,11 +562,6 @@
                     places, weight_rows, shards, mem_count, group_size, 0, group_size
                 )
                 due[stage + 1] = picked
-                picked, _ = lax.optimization_barrier((picked, latest))
-                latest = exchange(picked)
-                due[stage + half_way - 1] = latest
-                for index in range(SPLIT):
-                    obs_parts[index].append((latest, index * part * slots))
             else:
                 for index in range(SPLIT):
                     picked = pick(
@@ -554,6 +576,9 @@
     results = []
     for index in range(SPLIT):
         start = first_row + index * part
+        if results:
+            start, results[-1] = lax.optimization_barrier((start, results[-1]))
+            results[-1] = exchange(results[-1])
         result = analyse(
             (start * slots).reshape(1),
             lax.dynamic_slice_in_dim(prior_weight, start, part, 0),
@@ -562,7 +587,8 @@
             obs_parts[index],
             slots,
         )
-        results.append(exchange(result))
+        results.append(result)
+    results[-1] = exchange(results[-1])
     back = jnp.concatenate(results, axis=1)
     return jnp.transpose(back.reshape(regions_dev, members_dev, points), (1, 0, 2))
 

time: 272 us -> 251 us (0.923)
  Pallas kernels: 76.2 us -> 63.4 us
  local copies, waits for them, and re-layouts: 28.8 us -> 19.1 us
  waiting for transfers between devices: 97.8 us -> 102 us
    pallas_call x2, Pallas kernels: 65 us -> 50.5 us  [analyse(): pl.pallas_call(functools.partial(analysis_kernel, [offset for _, offset i...]
    all_to_all x5, waiting for transfers between devices: 30.1 us -> 42 us  [exchange(): lax.all_to_all(picked, 'mem', split_axis=0, concat_axis=0, tiled=True)]
    unnamed x74 -> x56, local copies, waits for them, and re-layouts: 18.6 us -> 9.6 us
    ppermute x6, waiting for transfers between devices: 21.9 us -> 13.4 us  [ring_step(): lax.ppermute(ahead, 'space', forward)]
  transfers between devices with their start and end apart: 28 -> 28, of which waited for: 15 -> 15; matrix products, arithmetic and copies ran while one was open for 3% -> 3% of each run, Pallas kernels for 26% -> 25%
where the time goes in v1:
time: 251 us; the launch traced here: 250 us
  waiting for transfers between devices  102 us (41%)
  Pallas kernels  63.4 us (25%)
  starting transfers between devices  46.6 us (19%)
  local copies, waits for them, and re-layouts  19.1 us (8%)
  blocking collectives  17.5 us (7%)
    pallas_call x2, Pallas kernels, analyse(): pl.pallas_call(functools.partial(analysis_kernel, [offset for _, offset i...  50.5 us
    all_to_all x5, waiting for transfers between devices, exchange(): lax.all_to_all(picked, 'mem', split_axis=0, concat_axis=0, tiled=True)  42 us
    ppermute x4, waiting for transfers between devices, body(): tied['ahead'] = lax.ppermute(rows_ahead[-1], 'space', forward)  35.1 us
    all_to_all x5, starting transfers between devices, exchange(): lax.all_to_all(picked, 'mem', split_axis=0, concat_axis=0, tiled=True)  21.1 us
    all_to_all x1, blocking collectives, exchange(): lax.all_to_all(picked, 'mem', split_axis=0, concat_axis=0, tiled=True)  17.5 us
    ppermute x6, waiting for transfers between devices, ring_step(): lax.ppermute(ahead, 'space', forward)  13.4 us
    ppermute x6, starting transfers between devices, ring_step(): lax.ppermute(ahead, 'space', forward)  10.4 us
    pallas_call x3, Pallas kernels, pick(): pl.pallas_call(functools.partial(pick_kernel, layout, group_size, first_r...  9.66 us
  transfers between devices with their start and end apart: 28, of which 15 were waited for; matrix products, arithmetic and copies ran while one was open for 3% of the time, Pallas kernels for 25%

profile of v1, /device:TPU:0, one launch (start us, length us, event | category | flops | bytes accessed | tf_op | source)
XLA Modules:
  0.0 250.3 jit_solution(5361089211923970583)
XLA Ops:
  1.8 3.0 %collective-permute-start.2 = (bf16[64,32,128]{2,1,0:T(8,128)(2,1)S(1)}, bf16[64,32,128]{2,1,0:T(8,128)(2,1)S(1)}, u32[]{:S(2)}, u32[]{:S(2)}) collective-permute-start(bf16[64,32,128]{2,1,0:T(8,128)(2,1)S(1)} %bitcast.18), channel_id=1, source_target_pairs={{4,12},{12,20},{20,28},{28,24},{24,16},{16,8},{8,0},{0,4},{5,13},{... | collective-permute-start | bytes 1572872 | tf_op jit(solution)/shard_map/ppermute | solution.py:499
  5.0 1.9 collective-permute-start
  7.4 10.8 %collective-permute-done.rest_1_ = f32[64,256]{1,0:T(8,128)S(1)} collective-permute-done((f32[64,256]{1,0:T(8,128)S(1)}, f32[64,256]{1,0:T(8,128)S(1)}, u32[]{:S(2)}, u32[]{:S(2)}) %collective-permute-start) | collective-permute-done | bytes 65568 | tf_op jit(solution)/shard_map/ppermute | solution.py:525
  19.6 1.6 collective-permute-start.6
  21.7 2.5 %copy.15 = bf16[64,64,256]{2,1,0:T(8,128)(2,1)} copy(bf16[64,64,256]{2,0,1:T(8,128)(2,1)S(1)} %bitcast.23) | data formatting | bytes 4194304 | tf_op jit(solution)/shard_map/transpose | solution.py:545
  24.2 4.6 %all-to-all-start = ((bf16[4,16,64,256]{3,2,1,0:T(8,128)(2,1)}), bf16[4,16,64,256]{3,2,1,0:T(8,128)(2,1)}, u32[]{:S(2)}, u32[]{:S(2)}) async-start(bf16[4,16,64,256]{3,2,1,0:T(8,128)(2,1)} %bitcast.21), calls=%async_computation | async-start | bytes 4194304 | tf_op jit(solution)/shard_map/all_to_all | solution.py:509
  28.8 1.6 collective-permute-start.4
  30.9 2.6 %collective-permute-done.4.rest_2_ = f32[64,256]{1,0:T(8,128)S(1)} collective-permute-done((f32[64,256]{1,0:T(8,128)S(1)}, f32[64,256]{1,0:T(8,128)S(1)}, u32[]{:S(2)}, u32[]{:S(2)}) %collective-permute-start.4) | collective-permute-done | bytes 65568 | tf_op jit(solution)/shard_map/ppermute | solution.py:525
  34.8 1.6 collective-permute-start.10
  36.9 1.6 collective-permute-start.8
  38.9 11.0 %collective-permute-done.8.rest_3_ = f32[64,256]{1,0:T(8,128)S(1)} collective-permute-done((f32[64,256]{1,0:T(8,128)S(1)}, f32[64,256]{1,0:T(8,128)S(1)}, u32[]{:S(2)}, u32[]{:S(2)}) %collective-permute-start.8) | collective-permute-done | bytes 65568 | tf_op jit(solution)/shard_map/ppermute | solution.py:525
  51.3 1.6 collective-permute-start.14
  57.2 1.6 collective-permute-start.16
  60.2 10.6 %collective-permute-done.16.rest_4_ = f32[64,256]{1,0:T(8,128)} collective-permute-done((f32[64,256]{1,0:T(8,128)}, f32[64,256]{1,0:T(8,128)}, u32[]{:S(2)}, u32[]{:S(2)}) %collective-permute-start.16) | collective-permute-done | bytes 65568 | tf_op jit(solution)/shard_map/ppermute | solution.py:525
  70.8 3.2 %shard_map.82.scale_ref.weight_ref = f32[512,256]{1,0:T(8,128)} custom-call(s32[512]{0:T(512)} %fusion.3.ids_ref, f32[512]{0:T(512)} %reshape.24.local_ref, f32[64,256]{1,0:T(8,128)} %copy-done.14, f32[64,256]{1,0:T(8,128)} %copy-done.15, f32[64,256]{1,0:T(8,128)} %copy-done.17, f32[64,256]{1,0:T(8,128)} %copy-done.19, ...), custom_call_target="tpu_custom_call" | custom-call | tf_op jit(solution)/shard_map/pallas_call | solution.py:54
  74.1 1.6 collective-permute-start.17
  80.0 2.8 %shard_map.83 = bf16[4,128,32,128]{3,2,1,0:T(8,128)(2,1)S(1)} custom-call(s32[512]{0:T(512)S(1)} %copy-done.10, f32[512,256]{1,0:T(8,128)S(1)} %copy-done.2, bf16[64,32,128]{2,1,0:T(8,128)(2,1)S(1)} %bitcast.20, bf16[64,32,128]{2,1,0:T(8,128)(2,1)S(1)} %copy-done.7, bf16[64,32,128]{2,1,0:T(8,128)(2,1)} %collective-permute-done.6.rest_2_, ...), custom_call_target="tpu_custom_call" | custom-call | flops 2097152 | bytes 16777216 | tf_op jit(solution)/shard_map/pallas_call | solution.py:94
  82.8 2.0 copy-done.1
  87.0 4.9 %all-to-all-start.1 = ((bf16[4,128,32,128]{3,2,1,0:T(8,128)(2,1)}), bf16[4,128,32,128]{3,2,1,0:T(8,128)(2,1)}, u32[]{:S(2)}, u32[]{:S(2)}) async-start(bf16[4,128,32,128]{3,2,1,0:T(8,128)(2,1)} %copy-done.1), calls=%async_computation.1 | async-start | bytes 8388608 | tf_op jit(solution)/shard_map/all_to_all | solution.py:509
  93.9 12.4 %collective-permute-done.19.rest_3_ = bf16[64,32,128]{2,1,0:T(8,128)(2,1)S(1)} collective-permute-done((bf16[64,32,128]{2,1,0:T(8,128)(2,1)}, bf16[64,32,128]{2,1,0:T(8,128)(2,1)S(1)}, u32[]{:S(2)}, u32[]{:S(2)}) %collective-permute-start.19) | collective-permute-done | bytes 524320 | tf_op jit(solution)/shard_map/ppermute | solution.py:499
  109.1 5.5 %collective-permute-done.21.rest_4_ = bf16[32,32,128]{2,1,0:T(8,128)(2,1)S(1)} collective-permute-done((bf16[32,32,128]{2,1,0:T(8,128)(2,1)S(1)}, bf16[32,32,128]{2,1,0:T(8,128)(2,1)S(1)}, u32[]{:S(2)}, u32[]{:S(2)}) %collective-permute-start.21) | collective-permute-done | bytes 262176 | tf_op jit(solution)/shard_map/ppermute | solution.py:504
  115.3 3.5 %shard_map.84 = bf16[4,64,32,128]{3,2,1,0:T(8,128)(2,1)} custom-call(s32[512]{0:T(512)S(1)} %copy-done.11, f32[512,256]{1,0:T(8,128)S(1)} %copy-done.3, bf16[64,32,128]{2,1,0:T(8,128)(2,1)S(1)} %bitcast.16, bf16[64,32,128]{2,1,0:T(8,128)(2,1)S(1)} %collective-permute-done.14.rest_1_, bf16[64,32,128]{2,1,0:T(8,128)(2,1)} %collective-permute-done.17.rest_2_, ...), custom_call_target="tpu_custom_call" | custom-call | flops 1048576 | bytes 12582912 | tf_op jit(solution)/shard_map/pallas_call | solution.py:94
  119.5 20.6 %all-to-all-done.1.rest_1_ = bf16[4,128,32,128]{3,2,1,0:T(8,128)(2,1)} async-done(((bf16[4,128,32,128]{3,2,1,0:T(8,128)(2,1)}), bf16[4,128,32,128]{3,2,1,0:T(8,128)(2,1)}, u32[]{:S(2)}, u32[]{:S(2)}) %all-to-all-start.1) | async-done | bytes 4194336 | tf_op jit(solution)/shard_map/all_to_all | solution.py:509
  140.1 4.5 %all-to-all-start.2 = ((bf16[4,64,32,128]{3,2,1,0:T(8,128)(2,1)}), bf16[4,64,32,128]{3,2,1,0:T(8,128)(2,1)}, u32[]{:S(2)}, u32[]{:S(2)}) async-start(bf16[4,64,32,128]{3,2,1,0:T(8,128)(2,1)} %shard_map.84), calls=%async_computation.2 | async-start | bytes 4194304 | tf_op jit(solution)/shard_map/all_to_all | solution.py:509
  145.5 3.4 %shard_map.86 = bf16[4,64,32,128]{3,2,1,0:T(8,128)(2,1)} custom-call(s32[512]{0:T(512)S(1)} %copy-done.11, f32[512,256]{1,0:T(8,128)S(1)} %copy-done.3, bf16[64,32,128]{2,1,0:T(8,128)(2,1)S(1)} %bitcast.17, bf16[64,32,128]{2,1,0:T(8,128)(2,1)S(1)} %collective-permute-done.14.rest_1_, bf16[64,32,128]{2,1,0:T(8,128)(2,1)} %collective-permute-done.17.rest_2_, ...), custom_call_target="tpu_custom_call" | custom-call | flops 1048576 | bytes 12582912 | tf_op jit(solution)/shard_map/pallas_call | solution.py:94
  148.9 21.4 %all-to-all-done.2.rest_2_ = bf16[4,64,32,128]{3,2,1,0:T(8,128)(2,1)} async-done(((bf16[4,64,32,128]{3,2,1,0:T(8,128)(2,1)}), bf16[4,64,32,128]{3,2,1,0:T(8,128)(2,1)}, u32[]{:S(2)}, u32[]{:S(2)}) %all-to-all-start.2) | async-done | bytes 2097184 | tf_op jit(solution)/shard_map/all_to_all | solution.py:509
  170.3 3.6 %all-to-all-start.4 = ((bf16[4,64,32,128]{3,2,1,0:T(8,128)(2,1)}), bf16[4,64,32,128]{3,2,1,0:T(8,128)(2,1)S(1)}, u32[]{:S(2)}, u32[]{:S(2)}) async-start(bf16[4,64,32,128]{3,2,1,0:T(8,128)(2,1)} %shard_map.86), calls=%async_computation.4 | async-start | bytes 4194304 | tf_op jit(solution)/shard_map/all_to_all | solution.py:509
  174.3 25.7 %shard_map.85 = bf16[4,8,64,256]{3,2,1,0:T(8,128)(2,1)} custom-call(s32[1]{0:T(128)} %bitcast.first_ref, f32[8,256]{1,0:T(8,128)S(1)} %constant_dynamic-slice_fusion.1.prior_ref, f32[8,256,128]{2,1,0:T(8,128)S(1)} %broadcast_in_dim.40.column_ref, f32[512,256]{1,0:T(8,128)S(1)} %copy-done.3, bf16[4,16,64,256]{3,2,1,0:T(8,128)(2,1)} %all-to-all-done.rest_0_, ...), custom_call_target="tpu_custom_call" | custom-call | flops 10737418240 | bytes 6291456 | tf_op jit(solution)/shard_map/pallas_call | solution.py:433
  201.4 3.5 %all-to-all-start.3 = ((bf16[4,8,64,256]{3,2,1,0:T(8,128)(2,1)}), bf16[4,8,64,256]{3,2,1,0:T(8,128)(2,1)S(1)}, u32[]{:S(2)}, u32[]{:S(2)}) async-start(bf16[4,8,64,256]{3,2,1,0:T(8,128)(2,1)} %shard_map.85), calls=%async_computation.3 | async-start | bytes 2097152 | tf_op jit(solution)/shard_map/all_to_all | solution.py:509
  205.2 24.8 %shard_map.87 = bf16[4,8,64,256]{3,2,1,0:T(8,128)(2,1)S(1)} custom-call(s32[1]{0:T(128)} %bitcast.5.first_ref, f32[8,256]{1,0:T(8,128)S(1)} %constant_dynamic-slice_fusion.prior_ref, f32[8,256,128]{2,1,0:T(8,128)S(1)} %broadcast_in_dim.44.column_ref, f32[512,256]{1,0:T(8,128)S(1)} %copy-done.3, bf16[4,16,64,256]{3,2,1,0:T(8,128)(2,1)} %all-to-all-done.rest_0_, ...), custom_call_target="tpu_custom_call" | custom-call | flops 10737418240 | bytes 6291456 | tf_op jit(solution)/shard_map/pallas_call | solution.py:433
  230.1 17.5 %all_to_all.30 = bf16[4,8,64,256]{3,2,1,0:T(8,128)(2,1)S(1)} all-to-all(bf16[4,8,64,256]{3,2,1,0:T(8,128)(2,1)S(1)} %shard_map.87), channel_id=1, replica_groups=mesh['space'=8,'mem'=4] {'mem'}, dimensions={0} | all-to-all | bytes 2097152 | tf_op jit(solution)/shard_map/all_to_all | solution.py:509
  247.8 2.5 %copy.24 = bf16[64,64,256]{2,0,1:T(8,128)(2,1)} copy(bf16[64,64,256]{2,1,0:T(8,128)(2,1)S(1)} %bitcast.22) | data formatting | bytes 4194304 | tf_op jit(solution)/shard_map/reshape | solution.py:593
  (105 shorter events, 29.6 us)
Async XLA Ops:
  0.0 173.9 %copy-start = (f32[64,256]{1,0:T(8,128)S(1)}, f32[64,256]{1,0:T(8,128)}, u32[]{:S(2)}) copy-start(f32[64,256]{1,0:T(8,128)} %param.15) | copy-start | bytes 196612
  1.8 17.8 %collective-permute-start.2 = (bf16[64,32,128]{2,1,0:T(8,128)(2,1)S(1)}, bf16[64,32,128]{2,1,0:T(8,128)(2,1)S(1)}, u32[]{:S(2)}, u32[]{:S(2)}) collective-permute-start(bf16[64,32,128]{2,1,0:T(8,128)(2,1)S(1)} %bitcast.18), channel_id=1, source_target_pairs={{4,12},{12,20},{20,28},{28,24},{24,16},{16,8},{8,0},{0,4},{5,13},{... | collective-permute-start | bytes 1572872 | tf_op jit(solution)/shard_map/ppermute | solution.py:499
  4.8 14.8 %collective-permute-start.3 = (bf16[64,32,128]{2,1,0:T(8,128)(2,1)S(1)}, bf16[64,32,128]{2,1,0:T(8,128)(2,1)S(1)}, u32[]{:S(2)}, u32[]{:S(2)}) collective-permute-start(bf16[64,32,128]{2,1,0:T(8,128)(2,1)S(1)} %bitcast.19), channel_id=1, source_target_pairs={{12,4},{20,12},{28,20},{24,28},{16,24},{8,16},{0,8},{4,0},{13,5},{... | collective-permute-start | bytes 1572872 | tf_op jit(solution)/shard_map/ppermute | solution.py:499
  5.0 13.2 %collective-permute-start = (f32[64,256]{1,0:T(8,128)S(1)}, f32[64,256]{1,0:T(8,128)S(1)}, u32[]{:S(2)}, u32[]{:S(2)}) collective-permute-start(f32[64,256]{1,0:T(8,128)S(1)} %constant_dynamic-update-slice_fusion.rest_0_), channel_id=1, source_target_pairs={{4,12},{12,20},{20,28},{28,24},{24,16},{16,8},{8,0},{0,4},{5,13},{... | collective-permute-start | bytes 196616 | tf_op jit(solution)/shard_map/ppermute | solution.py:525
  6.9 12.7 %collective-permute-start.1 = (f32[64,256]{1,0:T(8,128)S(1)}, f32[64,256]{1,0:T(8,128)S(1)}, u32[]{:S(2)}, u32[]{:S(2)}) collective-permute-start(f32[64,256]{1,0:T(8,128)S(1)} %constant_dynamic-update-slice_fusion.rest_0_), channel_id=1, source_target_pairs={{12,4},{20,12},{28,20},{24,28},{16,24},{8,16},{0,8},{4,0},{13,5},{... | collective-permute-start | bytes 196616 | tf_op jit(solution)/shard_map/ppermute | solution.py:527
  19.6 15.2 %collective-permute-start.6 = (bf16[64,32,128]{2,1,0:T(8,128)(2,1)S(1)}, bf16[64,32,128]{2,1,0:T(8,128)(2,1)}, u32[]{:S(2)}, u32[]{:S(2)}) collective-permute-start(bf16[64,32,128]{2,1,0:T(8,128)(2,1)S(1)} %collective-permute-done.2.rest_1_), channel_id=1, source_target_pairs={{4,12},{12,20},{20,28},{28,24},{24,16},{16,8},{8,0},{0,4},{5,13},{... | collective-permute-start | bytes 1572872 | tf_op jit(solution)/shard_map/ppermute | solution.py:499
  21.2 13.6 %collective-permute-start.7 = (bf16[64,32,128]{2,1,0:T(8,128)(2,1)S(1)}, bf16[64,32,128]{2,1,0:T(8,128)(2,1)}, u32[]{:S(2)}, u32[]{:S(2)}) collective-permute-start(bf16[64,32,128]{2,1,0:T(8,128)(2,1)S(1)} %collective-permute-done.3.rest_8_), channel_id=1, source_target_pairs={{12,4},{20,12},{28,20},{24,28},{16,24},{8,16},{0,8},{4,0},{13,5},{... | collective-permute-start | bytes 1572872 | tf_op jit(solution)/shard_map/ppermute | solution.py:499
  24.2 32.7 %copy-start.24 = (f32[64,8]{0,1:T(8,128)S(1)}, f32[64,8]{0,1:T(8,128)}, u32[]{:S(2)}) copy-start(f32[64,8]{0,1:T(8,128)} %param.14) | copy-start | bytes 6148
  24.2 32.7 %copy-start.25 = (s32[64]{0:T(128)S(1)}, s32[64]{0:T(128)}, u32[]{:S(2)}) copy-start(s32[64]{0:T(128)} %param.13) | copy-start | bytes 772
  24.2 32.7 %copy-start.23 = (s32[64,8]{0,1:T(8,128)S(1)}, s32[64,8]{0,1:T(8,128)}, u32[]{:S(2)}) copy-start(s32[64,8]{0,1:T(8,128)} %param.12) | copy-start | bytes 6148
  24.2 49.8 %all-to-all-start = ((bf16[4,16,64,256]{3,2,1,0:T(8,128)(2,1)}), bf16[4,16,64,256]{3,2,1,0:T(8,128)(2,1)}, u32[]{:S(2)}, u32[]{:S(2)}) async-start(bf16[4,16,64,256]{3,2,1,0:T(8,128)(2,1)} %bitcast.21), calls=%async_computation | async-start | bytes 4194304 | tf_op jit(solution)/shard_map/all_to_all | solution.py:509
  28.8 4.7 %collective-permute-start.4 = (f32[64,256]{1,0:T(8,128)S(1)}, f32[64,256]{1,0:T(8,128)S(1)}, u32[]{:S(2)}, u32[]{:S(2)}) collective-permute-start(f32[64,256]{1,0:T(8,128)S(1)} %collective-permute-done.rest_1_), channel_id=1, source_target_pairs={{4,12},{12,20},{20,28},{28,24},{24,16},{16,8},{8,0},{0,4},{5,13},{... | collective-permute-start | bytes 196616 | tf_op jit(solution)/shard_map/ppermute | solution.py:525
  30.5 4.4 %collective-permute-start.5 = (f32[64,256]{1,0:T(8,128)S(1)}, f32[64,256]{1,0:T(8,128)S(1)}, u32[]{:S(2)}, u32[]{:S(2)}) collective-permute-start(f32[64,256]{1,0:T(8,128)S(1)} %collective-permute-done.1.rest_7_), channel_id=1, source_target_pairs={{12,4},{20,12},{28,20},{24,28},{16,24},{8,16},{0,8},{4,0},{13,5},{... | collective-permute-start | bytes 196616 | tf_op jit(solution)/shard_map/ppermute | solution.py:527
  34.8 16.4 %collective-permute-start.10 = (bf16[64,32,128]{2,1,0:T(8,128)(2,1)}, bf16[64,32,128]{2,1,0:T(8,128)(2,1)S(1)}, u32[]{:S(2)}, u32[]{:S(2)}) collective-permute-start(bf16[64,32,128]{2,1,0:T(8,128)(2,1)} %collective-permute-done.6.rest_2_), channel_id=1, source_target_pairs={{4,12},{12,20},{20,28},{28,24},{24,16},{16,8},{8,0},{0,4},{5,13},{... | collective-permute-start | bytes 1572872 | tf_op jit(solution)/shard_map/ppermute | solution.py:499
  36.5 14.8 %collective-permute-start.11 = (bf16[64,32,128]{2,1,0:T(8,128)(2,1)}, bf16[64,32,128]{2,1,0:T(8,128)(2,1)S(1)}, u32[]{:S(2)}, u32[]{:S(2)}) collective-permute-start(bf16[64,32,128]{2,1,0:T(8,128)(2,1)} %collective-permute-done.7.rest_7_), channel_id=1, source_target_pairs={{12,4},{20,12},{28,20},{24,28},{16,24},{8,16},{0,8},{4,0},{13,5},{... | collective-permute-start | bytes 1572872 | tf_op jit(solution)/shard_map/ppermute | solution.py:499
  36.9 13.0 %collective-permute-start.8 = (f32[64,256]{1,0:T(8,128)S(1)}, f32[64,256]{1,0:T(8,128)S(1)}, u32[]{:S(2)}, u32[]{:S(2)}) collective-permute-start(f32[64,256]{1,0:T(8,128)S(1)} %collective-permute-done.4.rest_2_), channel_id=1, source_target_pairs={{4,12},{12,20},{20,28},{28,24},{24,16},{16,8},{8,0},{0,4},{5,13},{... | collective-permute-start | bytes 196616 | tf_op jit(solution)/shard_map/ppermute | solution.py:525
  38.5 12.8 %collective-permute-start.9 = (f32[64,256]{1,0:T(8,128)S(1)}, f32[64,256]{1,0:T(8,128)S(1)}, u32[]{:S(2)}, u32[]{:S(2)}) collective-permute-start(f32[64,256]{1,0:T(8,128)S(1)} %collective-permute-done.5.rest_6_), channel_id=1, source_target_pairs={{12,4},{20,12},{28,20},{24,28},{16,24},{8,16},{0,8},{4,0},{13,5},{... | collective-permute-start | bytes 196616 | tf_op jit(solution)/shard_map/ppermute | solution.py:527
  51.3 22.8 %collective-permute-start.14 = (bf16[64,32,128]{2,1,0:T(8,128)(2,1)S(1)}, bf16[64,32,128]{2,1,0:T(8,128)(2,1)S(1)}, u32[]{:S(2)}, u32[]{:S(2)}) collective-permute-start(bf16[64,32,128]{2,1,0:T(8,128)(2,1)S(1)} %bitcast.14), channel_id=1, source_target_pairs={{4,12},{12,20},{20,28},{28,24},{24,16},{16,8},{8,0},{0,4},{5,13},{... | collective-permute-start | bytes 1572872 | tf_op jit(solution)/shard_map/ppermute | solution.py:499
  52.9 21.1 %collective-permute-start.15 = (bf16[64,32,128]{2,1,0:T(8,128)(2,1)S(1)}, bf16[64,32,128]{2,1,0:T(8,128)(2,1)S(1)}, u32[]{:S(2)}, u32[]{:S(2)}) collective-permute-start(bf16[64,32,128]{2,1,0:T(8,128)(2,1)S(1)} %bitcast.15), channel_id=1, source_target_pairs={{12,4},{20,12},{28,20},{24,28},{16,24},{8,16},{0,8},{4,0},{13,5},{... | collective-permute-start | bytes 1572872 | tf_op jit(solution)/shard_map/ppermute | solution.py:499
  54.1 19.9 %collective-permute-start.12 = (bf16[32,32,128]{2,1,0:T(8,128)(2,1)}, bf16[32,32,128]{2,1,0:T(8,128)(2,1)S(1)}, u32[]{:S(2)}, u32[]{:S(2)}) collective-permute-start(bf16[32,32,128]{2,1,0:T(8,128)(2,1)} %slice.20), channel_id=1, source_target_pairs={{4,12},{12,20},{20,28},{28,24},{24,16},{16,8},{8,0},{0,4},{5,13},{... | collective-permute-start | bytes 786440 | tf_op jit(solution)/shard_map/ppermute | solution.py:504
  56.5 17.6 %collective-permute-start.13 = (bf16[32,32,128]{2,1,0:T(8,128)(2,1)}, bf16[32,32,128]{2,1,0:T(8,128)(2,1)}, u32[]{:S(2)}, u32[]{:S(2)}) collective-permute-start(bf16[32,32,128]{2,1,0:T(8,128)(2,1)} %slice.21), channel_id=1, source_target_pairs={{12,4},{20,12},{28,20},{24,28},{16,24},{8,16},{0,8},{4,0},{13,5},{... | collective-permute-start | bytes 786440 | tf_op jit(solution)/shard_map/ppermute | solution.py:505
  57.2 13.6 %collective-permute-start.16 = (f32[64,256]{1,0:T(8,128)}, f32[64,256]{1,0:T(8,128)}, u32[]{:S(2)}, u32[]{:S(2)}) collective-permute-start(f32[64,256]{1,0:T(8,128)} %copy-done.19), channel_id=1, source_target_pairs={{4,12},{12,20},{20,28},{28,24},{24,16},{16,8},{8,0},{0,4},{5,13},{... | collective-permute-start | bytes 196616 | tf_op jit(solution)/shard_map/ppermute | solution.py:525
  74.1 11.6 %collective-permute-start.17 = (bf16[64,32,128]{2,1,0:T(8,128)(2,1)S(1)}, bf16[64,32,128]{2,1,0:T(8,128)(2,1)}, u32[]{:S(2)}, u32[]{:S(2)}) collective-permute-start(bf16[64,32,128]{2,1,0:T(8,128)(2,1)S(1)} %collective-permute-done.14.rest_1_), channel_id=1, source_target_pairs={{4,12},{12,20},{20,28},{28,24},{24,16},{16,8},{8,0},{0,4},{5,13},{... | collective-permute-start | bytes 1572872 | tf_op jit(solution)/shard_map/ppermute | solution.py:499
  75.7 11.3 %collective-permute-start.18 = (bf16[64,32,128]{2,1,0:T(8,128)(2,1)S(1)}, bf16[64,32,128]{2,1,0:T(8,128)(2,1)}, u32[]{:S(2)}, u32[]{:S(2)}) collective-permute-start(bf16[64,32,128]{2,1,0:T(8,128)(2,1)S(1)} %collective-permute-done.15.rest_8_), channel_id=1, source_target_pairs={{12,4},{20,12},{28,20},{24,28},{16,24},{8,16},{0,8},{4,0},{13,5},{... | collective-permute-start | bytes 1572872 | tf_op jit(solution)/shard_map/ppermute | solution.py:499
  87.0 53.1 %all-to-all-start.1 = ((bf16[4,128,32,128]{3,2,1,0:T(8,128)(2,1)}), bf16[4,128,32,128]{3,2,1,0:T(8,128)(2,1)}, u32[]{:S(2)}, u32[]{:S(2)}) async-start(bf16[4,128,32,128]{3,2,1,0:T(8,128)(2,1)} %copy-done.1), calls=%async_computation.1 | async-start | bytes 8388608 | tf_op jit(solution)/shard_map/all_to_all | solution.py:509
  91.9 14.5 %collective-permute-start.19 = (bf16[64,32,128]{2,1,0:T(8,128)(2,1)}, bf16[64,32,128]{2,1,0:T(8,128)(2,1)S(1)}, u32[]{:S(2)}, u32[]{:S(2)}) collective-permute-start(bf16[64,32,128]{2,1,0:T(8,128)(2,1)} %collective-permute-done.17.rest_2_), channel_id=1, source_target_pairs={{4,12},{12,20},{20,28},{28,24},{24,16},{16,8},{8,0},{0,4},{5,13},{... | collective-permute-start | bytes 1572872 | tf_op jit(solution)/shard_map/ppermute | solution.py:499
  92.8 14.2 %collective-permute-start.20 = (bf16[64,32,128]{2,1,0:T(8,128)(2,1)}, bf16[64,32,128]{2,1,0:T(8,128)(2,1)S(1)}, u32[]{:S(2)}, u32[]{:S(2)}) collective-permute-start(bf16[64,32,128]{2,1,0:T(8,128)(2,1)} %collective-permute-done.18.rest_7_), channel_id=1, source_target_pairs={{12,4},{20,12},{28,20},{24,28},{16,24},{8,16},{0,8},{4,0},{13,5},{... | collective-permute-start | bytes 1572872 | tf_op jit(solution)/shard_map/ppermute | solution.py:499
  107.0 7.7 %collective-permute-start.21 = (bf16[32,32,128]{2,1,0:T(8,128)(2,1)S(1)}, bf16[32,32,128]{2,1,0:T(8,128)(2,1)S(1)}, u32[]{:S(2)}, u32[]{:S(2)}) collective-permute-start(bf16[32,32,128]{2,1,0:T(8,128)(2,1)S(1)} %slice.22), channel_id=1, source_target_pairs={{4,12},{12,20},{20,28},{28,24},{24,16},{16,8},{8,0},{0,4},{5,13},{... | collective-permute-start | bytes 786440 | tf_op jit(solution)/shard_map/ppermute | solution.py:504
  107.9 7.4 %collective-permute-start.22 = (bf16[32,32,128]{2,1,0:T(8,128)(2,1)S(1)}, bf16[32,32,128]{2,1,0:T(8,128)(2,1)S(1)}, u32[]{:S(2)}, u32[]{:S(2)}) collective-permute-start(bf16[32,32,128]{2,1,0:T(8,128)(2,1)S(1)} %slice.23), channel_id=1, source_target_pairs={{12,4},{20,12},{28,20},{24,28},{16,24},{8,16},{0,8},{4,0},{13,5},{... | collective-permute-start | bytes 786440 | tf_op jit(solution)/shard_map/ppermute | solution.py:505
  140.1 30.2 %all-to-all-start.2 = ((bf16[4,64,32,128]{3,2,1,0:T(8,128)(2,1)}), bf16[4,64,32,128]{3,2,1,0:T(8,128)(2,1)}, u32[]{:S(2)}, u32[]{:S(2)}) async-start(bf16[4,64,32,128]{3,2,1,0:T(8,128)(2,1)} %shard_map.84), calls=%async_computation.2 | async-start | bytes 4194304 | tf_op jit(solution)/shard_map/all_to_all | solution.py:509
  170.3 29.8 %all-to-all-start.4 = ((bf16[4,64,32,128]{3,2,1,0:T(8,128)(2,1)}), bf16[4,64,32,128]{3,2,1,0:T(8,128)(2,1)S(1)}, u32[]{:S(2)}, u32[]{:S(2)}) async-start(bf16[4,64,32,128]{3,2,1,0:T(8,128)(2,1)} %shard_map.86), calls=%async_computation.4 | async-start | bytes 4194304 | tf_op jit(solution)/shard_map/all_to_all | solution.py:509
  201.4 28.7 %all-to-all-start.3 = ((bf16[4,8,64,256]{3,2,1,0:T(8,128)(2,1)}), bf16[4,8,64,256]{3,2,1,0:T(8,128)(2,1)S(1)}, u32[]{:S(2)}, u32[]{:S(2)}) async-start(bf16[4,8,64,256]{3,2,1,0:T(8,128)(2,1)} %shard_map.85), calls=%async_computation.3 | async-start | bytes 2097152 | tf_op jit(solution)/shard_map/all_to_all | solution.py:509
  (22 other events, 191.8 us)
